TPU v7x, 32 devices: a whole 2x2x4 slice. The times are simulated.
32 devices in a mesh: layer: 4 (over y, core), tx: 2 (over x), ty: 4 (over z).
Axes of the slice: x: 2, y: 2, z: 4, core: 2. Of those that a mesh axis runs over, the one named last changes fastest.
Arguments:
- layers: float32 [4, 256, 2048], P('layer', 'tx', 'ty'), may hold values from -6 to 6
- wind: int32 [4, 2], P('layer'), may hold values from -128 to 128
- offsets: int32 [4, 9, 2], P('layer'), may hold values from -64 to 64
- weights: bfloat16 [9, 2, 256, 2048], P(None, None, 'tx', 'ty'), may hold values from -0.5 to 0.5
- sub_index: int32 [256, 2048], P('tx', 'ty'), may hold values from -1 to 255, as said below
Outputs:
- slopes: float32 [2, 9, 32, 256], P(None, None, 'tx', 'ty')
Inputs may be any that keep to these rules, and one draw needn't show every extreme that they name: sub_index[i, j] is -1 or j // 8.
All inputs are finite; a program needn't handle non-finite values.
Results may differ from a plain program's by a relative error of at most 0.0003.
Values sent between devices are 32-bit elements; how exact they have to be, the bound alone decides.
A program may use at most 256 MiB of HBM per device.

v0:
```python
import jax
import jax.numpy as jnp
from jax import lax
from jax.sharding import PartitionSpec as P

DIRS = 9
SUB = 8
HMAX = 2
FOOT = 64


def padded(cells, sides, width):
    for axis, dim in sides:
        count = lax.axis_size(axis)
        head = lax.slice_in_dim(cells, 0, width, axis=dim)
        tail = lax.slice_in_dim(cells, cells.shape[dim] - width, cells.shape[dim], axis=dim)
        cells = jnp.concatenate(
            [
                lax.ppermute(tail, axis, [(i, (i + 1) % count) for i in range(count)]),
                cells,
                lax.ppermute(head, axis, [((i + 1) % count, i) for i in range(count)]),
            ],
            axis=dim,
        )
    return cells


def shift_stack(extended, quotient, fraction, out_rows, out_cols):
    margin = HMAX + 1
    field = extended[0]
    start_row = margin - quotient[0, 0]
    start_col = margin - quotient[0, 1]
    corner_aa = lax.dynamic_slice(field, (start_row, start_col), (out_rows, out_cols))
    corner_ab = lax.dynamic_slice(field, (start_row, start_col - 1), (out_rows, out_cols))
    corner_ba = lax.dynamic_slice(field, (start_row - 1, start_col), (out_rows, out_cols))
    corner_bb = lax.dynamic_slice(field, (start_row - 1, start_col - 1), (out_rows, out_cols))
    frow = fraction[0, 0]
    fcol = fraction[0, 1]
    pieces = [
        (1.0 - frow) * ((1.0 - fcol) * corner_aa + fcol * corner_ab)
        + frow * ((1.0 - fcol) * corner_ba + fcol * corner_bb)
    ]
    return jnp.stack(pieces)


def on_device(layers, wind, offsets, weights, sub_index):
    count, rows, cols = layers.shape
    quotient = jnp.floor_divide(wind, 64)
    fraction = (wind - 64 * quotient).astype(jnp.float32) / 64.0
    rimmed = padded(layers, (("tx", 1), ("ty", 2)), HMAX + 1)
    shifted = shift_stack(rimmed, quotient, fraction, rows, cols)
    spread = padded(shifted, (("tx", 1), ("ty", 2)), FOOT)
    live = (sub_index >= 0).astype(jnp.float32)
    results = []
    for d in range(DIRS):
        start_row = FOOT + offsets[0, d, 0]
        start_col = FOOT + offsets[0, d, 1]
        total = lax.dynamic_slice(spread[0], (start_row, start_col), (rows, cols))
        masked = total * live
        terms = weights[d].astype(jnp.float32) * masked[None]
        results.append(terms.reshape(2, rows // SUB, SUB, cols // SUB, SUB).sum(axis=(2, 4)))
    local_slopes = jnp.stack(results, axis=1)
    return lax.psum(local_slopes, "layer")


def solution(mesh):
    placed = (
        P("layer", "tx", "ty"),
        P("layer", None),
        P("layer", None, None),
        P(None, None, "tx", "ty"),
        P("tx", "ty"),
    )
    return jax.shard_map(
        on_device, mesh=mesh, in_specs=placed, out_specs=P(None, None, "tx", "ty"), check_vma=False
    )
```

profile of v0, /device:TPU:0, one launch (start us, length us, event | category | flops | bytes accessed | tf_op | source)
XLA Modules:
  0.0 238.4 jit_solution(12341837292214623267)
XLA Ops:
  6.5 0.7 fusion.1
  7.3 2.9 %collective-permute-start.1 = (f32[1,3,512]{2,1,0:T(4,128)S(1)}, f32[1,3,512]{2,1,0:T(4,128)S(1)}, u32[]{:S(2)}, u32[]{:S(2)}) collective-permute-start(f32[1,3,512]{2,1,0:T(4,128)S(1)} %get-tuple-element.33), channel_id=1, source_target_pairs={{4,0},{0,4},{5,1},{1,5},{6,2},{2,6},{7,3},{3,7},{12,8},{8,12},{13,... | collective-permute-start | bytes 18440 | tf_op jit(solution)/shard_map/ppermute | solution.py:21
  10.2 0.1 collective-permute-start
  10.3 0.7 convert_multiply_fusion
  11.0 0.6 fusion.4
  11.5 0.6 fusion.3
  14.6 0.0 collective-permute-done.1
  14.6 0.0 collective-permute-done
  14.6 1.0 pad_maximum_fusion.7
  15.6 4.1 %collective-permute-start.3 = (f32[1,134,3]{2,1,0:T(8,128)S(1)}, f32[1,134,3]{2,1,0:T(8,128)S(1)}, u32[]{:S(2)}, u32[]{:S(2)}) collective-permute-start(f32[1,134,3]{2,1,0:T(8,128)S(1)} %get-tuple-element.29), channel_id=1, source_target_pairs={{1,0},{2,1},{3,2},{0,3},{5,4},{6,5},{7,6},{4,7},{9,8},{10,9},{11,1... | collective-permute-start | bytes 4832 | tf_op jit(solution)/shard_map/ppermute | solution.py:21
  19.7 0.0 collective-permute-start.2
  23.4 0.0 collective-permute-done.3
  23.4 2.4 %collective-permute-done.2 = f32[1,134,3]{2,1,0:T(8,128)S(1)} collective-permute-done((f32[1,134,3]{2,1,0:T(8,128)S(1)}, f32[1,134,3]{2,1,0:T(8,128)S(1)}, u32[]{:S(2)}, u32[]{:S(2)}) %collective-permute-start.2) | collective-permute-done | bytes 1640 | tf_op jit(solution)/shard_map/ppermute | solution.py:19
  25.8 1.1 pad_maximum_fusion.1
  26.9 1.6 multiply_add_fusion
  28.6 1.6 collective-permute-start.5
  30.1 0.5 collective-permute-start.4
  30.7 3.2 %slice_convert_fusion = (f32[1,2,128,512]{3,2,1,0:T(8,128)S(1)}, f32[1,2,128,512]{3,2,1,0:T(8,128)S(1)}, f32[1,2,128,512]{3,2,1,0:T(8,128)S(1)}, f32[1,2,128,512...) fusion(bf16[9,2,128,512]{3,2,1,0:T(8,128)(2,1)} %param.8), kind=kLoop, calls=%fused_computation.20 | loop fusion | flops 1179648 | bytes 7077888 | tf_op jit(solution)/shard_map/convert_element_type | solution.py:60
  33.9 0.0 collective-permute-done.5
  33.9 1.2 collective-permute-done.4
  35.1 0.6 copy-done.2
  35.7 0.8 pad_maximum_fusion.4
  36.5 1.9 collective-permute-start.7
  38.4 0.1 collective-permute-start.6
  38.5 0.7 fusion.2
  61.0 7.1 %reshape.200 = f32[2,16,8,64,8]{4,3,2,1,0:T(8,128)} reshape(f32[1,2,128,512]{3,2,1,0:T(8,128)} %get-tuple-element.16) | data formatting | bytes 1048576 | tf_op jit(solution)/shard_map/convert_element_type | solution.py:60
  68.1 7.0 %reshape.201 = f32[2,16,8,64,8]{4,3,2,1,0:T(8,128)} reshape(f32[1,2,128,512]{3,2,1,0:T(8,128)} %get-tuple-element.15) | data formatting | bytes 1048576 | tf_op jit(solution)/shard_map/convert_element_type | solution.py:60
  75.1 7.1 %reshape.202 = f32[2,16,8,64,8]{4,3,2,1,0:T(8,128)} reshape(f32[1,2,128,512]{3,2,1,0:T(8,128)} %get-tuple-element.14) | data formatting | bytes 1048576 | tf_op jit(solution)/shard_map/convert_element_type | solution.py:60
  82.2 6.1 %reshape.203 = f32[2,16,8,64,8]{4,3,2,1,0:T(8,128)} reshape(f32[1,2,128,512]{3,2,1,0:T(8,128)S(1)} %get-tuple-element.13) | data formatting | bytes 1048576 | tf_op jit(solution)/shard_map/convert_element_type | solution.py:60
  88.3 6.2 %reshape.204 = f32[2,16,8,64,8]{4,3,2,1,0:T(8,128)} reshape(f32[1,2,128,512]{3,2,1,0:T(8,128)S(1)} %get-tuple-element.12) | data formatting | bytes 1048576 | tf_op jit(solution)/shard_map/convert_element_type | solution.py:60
  94.5 6.1 %reshape.205 = f32[2,16,8,64,8]{4,3,2,1,0:T(8,128)} reshape(f32[1,2,128,512]{3,2,1,0:T(8,128)S(1)} %get-tuple-element.11) | data formatting | bytes 1048576 | tf_op jit(solution)/shard_map/convert_element_type | solution.py:60
  100.6 6.1 %reshape.206 = f32[2,16,8,64,8]{4,3,2,1,0:T(8,128)} reshape(f32[1,2,128,512]{3,2,1,0:T(8,128)S(1)} %get-tuple-element.10) | data formatting | bytes 1048576 | tf_op jit(solution)/shard_map/convert_element_type | solution.py:60
  106.7 6.1 %reshape.207 = f32[2,16,8,64,8]{4,3,2,1,0:T(8,128)} reshape(f32[1,2,128,512]{3,2,1,0:T(8,128)S(1)} %get-tuple-element.17) | data formatting | bytes 1048576 | tf_op jit(solution)/shard_map/convert_element_type | solution.py:60
  112.8 6.1 %reshape.208 = f32[2,16,8,64,8]{4,3,2,1,0:T(8,128)} reshape(f32[1,2,128,512]{3,2,1,0:T(8,128)S(1)} %get-tuple-element.9) | data formatting | bytes 1048576 | tf_op jit(solution)/shard_map/convert_element_type | solution.py:60
  118.9 0.0 collective-permute-done.7
  118.9 0.0 collective-permute-done.6
  118.9 1.2 pad_maximum_fusion
  120.2 0.1 bitcast_select_fusion
  120.4 0.7 bitcast_select_fusion.1
  121.1 3.7 %mul.215 = f32[16,8,64,8]{3,2,1,0:T(8,128)} reshape(f32[128,512]{1,0:T(8,128)S(1)} %get-tuple-element.25) | data formatting | bytes 524288 | tf_op jit(solution)/shard_map/mul | solution.py:60
  124.8 5.9 %multiply_reduce_fusion.8 = f32[2,16,64]{2,1,0:T(8,128)S(1)} fusion(f32[2,16,8,64,8]{4,3,2,1,0:T(8,128)} %reshape.200, f32[16,8,64,8]{3,2,1,0:T(8,128)} %mul.215), kind=kLoop, calls=%fused_computation.8 | loop fusion | flops 260096 | bytes 794624 | tf_op jit(solution)/shard_map/reduce_sum | solution.py:61
  130.7 3.7 %mul.219 = f32[16,8,64,8]{3,2,1,0:T(8,128)} reshape(f32[128,512]{1,0:T(8,128)S(1)} %get-tuple-element.24) | data formatting | bytes 524288 | tf_op jit(solution)/shard_map/mul | solution.py:60
  134.3 3.6 %mul.223 = f32[16,8,64,8]{3,2,1,0:T(8,128)} reshape(f32[128,512]{1,0:T(8,128)S(1)} %get-tuple-element.23) | data formatting | bytes 524288 | tf_op jit(solution)/shard_map/mul | solution.py:60
  137.9 3.6 %mul.227 = f32[16,8,64,8]{3,2,1,0:T(8,128)} reshape(f32[128,512]{1,0:T(8,128)S(1)} %get-tuple-element.22) | data formatting | bytes 524288 | tf_op jit(solution)/shard_map/mul | solution.py:60
  141.6 3.7 %mul.231 = f32[16,8,64,8]{3,2,1,0:T(8,128)} reshape(f32[128,512]{1,0:T(8,128)S(1)} %get-tuple-element.21) | data formatting | bytes 524288 | tf_op jit(solution)/shard_map/mul | solution.py:60
  145.2 3.6 %mul.235 = f32[16,8,64,8]{3,2,1,0:T(8,128)} reshape(f32[128,512]{1,0:T(8,128)S(1)} %get-tuple-element.20) | data formatting | bytes 524288 | tf_op jit(solution)/shard_map/mul | solution.py:60
  148.8 3.7 %mul.239 = f32[16,8,64,8]{3,2,1,0:T(8,128)} reshape(f32[128,512]{1,0:T(8,128)S(1)} %get-tuple-element.19) | data formatting | bytes 524288 | tf_op jit(solution)/shard_map/mul | solution.py:60
  152.5 3.6 %mul.243 = f32[16,8,64,8]{3,2,1,0:T(8,128)} reshape(f32[128,512]{1,0:T(8,128)S(1)} %get-tuple-element.18) | data formatting | bytes 524288 | tf_op jit(solution)/shard_map/mul | solution.py:60
  156.1 3.7 %mul.247 = f32[16,8,64,8]{3,2,1,0:T(8,128)} reshape(f32[128,512]{1,0:T(8,128)S(1)} %get-tuple-element.5) | data formatting | bytes 524288 | tf_op jit(solution)/shard_map/mul | solution.py:60
  159.8 6.0 %multiply_reduce_fusion.7 = f32[2,16,64]{2,1,0:T(8,128)S(1)} fusion(f32[2,16,8,64,8]{4,3,2,1,0:T(8,128)} %reshape.201, f32[16,8,64,8]{3,2,1,0:T(8,128)} %mul.219), kind=kLoop, calls=%fused_computation.7 | loop fusion | flops 260096 | bytes 794624 | tf_op jit(solution)/shard_map/reduce_sum | solution.py:61
  165.8 0.0 slice-start.6
  165.9 5.0 %multiply_reduce_fusion.6 = f32[2,16,64]{2,1,0:T(8,128)S(1)} fusion(f32[2,16,8,64,8]{4,3,2,1,0:T(8,128)} %reshape.202, f32[16,8,64,8]{3,2,1,0:T(8,128)S(1)} %copy-done.1), kind=kLoop, calls=%fused_computation.6 | loop fusion | flops 260096 | bytes 794624 | tf_op jit(solution)/shard_map/reduce_sum | solution.py:61
  170.9 5.0 %multiply_reduce_fusion.5 = f32[2,16,64]{2,1,0:T(8,128)S(1)} fusion(f32[2,16,8,64,8]{4,3,2,1,0:T(8,128)} %reshape.203, f32[16,8,64,8]{3,2,1,0:T(8,128)S(1)} %copy-done), kind=kLoop, calls=%fused_computation.5 | loop fusion | flops 260096 | bytes 794624 | tf_op jit(solution)/shard_map/reduce_sum | solution.py:61
  176.0 0.0 slice-start.5
  176.0 3.8 %multiply_reduce_fusion.4 = f32[2,16,64]{2,1,0:T(8,128)S(1)} fusion(f32[2,16,8,64,8]{4,3,2,1,0:T(8,128)S(1)} %bitcast.107, f32[16,8,64,8]{3,2,1,0:T(8,128)} %mul.231), kind=kLoop, calls=%fused_computation.4 | loop fusion | flops 260096 | bytes 794624 | tf_op jit(solution)/shard_map/reduce_sum | solution.py:61
  179.8 3.8 %multiply_reduce_fusion.3 = f32[2,16,64]{2,1,0:T(8,128)S(1)} fusion(f32[2,16,8,64,8]{4,3,2,1,0:T(8,128)S(1)} %bitcast.105, f32[16,8,64,8]{3,2,1,0:T(8,128)} %mul.235), kind=kLoop, calls=%fused_computation.3 | loop fusion | flops 260096 | bytes 794624 | tf_op jit(solution)/shard_map/reduce_sum | solution.py:61
  183.6 6.0 %multiply_reduce_fusion.2 = f32[2,16,64]{2,1,0:T(8,128)S(1)} fusion(f32[2,16,8,64,8]{4,3,2,1,0:T(8,128)} %reshape.206, f32[16,8,64,8]{3,2,1,0:T(8,128)} %mul.239), kind=kLoop, calls=%fused_computation.2 | loop fusion | flops 260096 | bytes 794624 | tf_op jit(solution)/shard_map/reduce_sum | solution.py:61
  189.6 0.0 slice-start.1
  189.6 3.8 %multiply_reduce_fusion.1 = f32[2,16,64]{2,1,0:T(8,128)S(1)} fusion(f32[2,16,8,64,8]{4,3,2,1,0:T(8,128)S(1)} %bitcast.103, f32[16,8,64,8]{3,2,1,0:T(8,128)} %mul.243), kind=kLoop, calls=%fused_computation.1 | loop fusion | flops 260096 | bytes 794624 | tf_op jit(solution)/shard_map/reduce_sum | solution.py:61
  193.4 3.6 %multiply_reduce_fusion = f32[2,16,64]{2,1,0:T(8,128)S(1)} fusion(f32[2,16,8,64,8]{4,3,2,1,0:T(8,128)S(1)} %bitcast.101, f32[16,8,64,8]{3,2,1,0:T(8,128)} %mul.247), kind=kLoop, calls=%fused_computation | loop fusion | flops 260096 | bytes 794624 | tf_op jit(solution)/shard_map/reduce_sum | solution.py:61
  197.1 0.7 copy-done.5
  197.7 0.0 all-reduce.2.cloned.1.call-update
  197.8 32.2 %all-reduce.2.cloned.1.call-done = f32[2,9,16,64]{3,2,1,0:T(8,128)} async-done(((f32[2,9,16,64]{3,2,1,0:T(8,128)}), f32[2,9,16,64]{3,2,1,0:T(8,128)}) %all-reduce.2.cloned.1.call-update) | async-done | bytes 73744 | tf_op jit(solution)/shard_map/psum | solution.py:63
  230.0 1.6 copy.15
  (40 shorter events, 0.1 us)
Async XLA Ops:
  6.5 32.0 %copy-start.6 = (s32[1,9,2]{1,2,0:T(2,128)S(1)}, s32[1,9,2]{1,2,0:T(2,128)}, u32[]{:S(2)}) copy-start(s32[1,9,2]{1,2,0:T(2,128)} %param.7) | copy-start | bytes 220
  6.5 223.4 %all-reduce.2.cloned.1.call-start = ((), (), s32[]{:S(2)}) async-start(), calls=%async_computation | async-start | bytes 294912 | tf_op jit(solution)/shard_map/psum | solution.py:63
  7.3 7.3 %collective-permute-start.1 = (f32[1,3,512]{2,1,0:T(4,128)S(1)}, f32[1,3,512]{2,1,0:T(4,128)S(1)}, u32[]{:S(2)}, u32[]{:S(2)}) collective-permute-start(f32[1,3,512]{2,1,0:T(4,128)S(1)} %get-tuple-element.33), channel_id=1, source_target_pairs={{4,0},{0,4},{5,1},{1,5},{6,2},{2,6},{7,3},{3,7},{12,8},{8,12},{13,... | collective-permute-start | bytes 18440 | tf_op jit(solution)/shard_map/ppermute | solution.py:21
  10.2 4.4 %collective-permute-start = (f32[1,3,512]{2,1,0:T(4,128)S(1)}, f32[1,3,512]{2,1,0:T(4,128)S(1)}, u32[]{:S(2)}, u32[]{:S(2)}) collective-permute-start(f32[1,3,512]{2,1,0:T(4,128)S(1)} %get-tuple-element.32), channel_id=1, source_target_pairs={{0,4},{4,0},{1,5},{5,1},{2,6},{6,2},{3,7},{7,3},{8,12},{12,8},{9,1... | collective-permute-start | bytes 18440 | tf_op jit(solution)/shard_map/ppermute | solution.py:19
  15.6 7.8 %collective-permute-start.3 = (f32[1,134,3]{2,1,0:T(8,128)S(1)}, f32[1,134,3]{2,1,0:T(8,128)S(1)}, u32[]{:S(2)}, u32[]{:S(2)}) collective-permute-start(f32[1,134,3]{2,1,0:T(8,128)S(1)} %get-tuple-element.29), channel_id=1, source_target_pairs={{1,0},{2,1},{3,2},{0,3},{5,4},{6,5},{7,6},{4,7},{9,8},{10,9},{11,1... | collective-permute-start | bytes 4832 | tf_op jit(solution)/shard_map/ppermute | solution.py:21
  19.7 6.1 %collective-permute-start.2 = (f32[1,134,3]{2,1,0:T(8,128)S(1)}, f32[1,134,3]{2,1,0:T(8,128)S(1)}, u32[]{:S(2)}, u32[]{:S(2)}) collective-permute-start(f32[1,134,3]{2,1,0:T(8,128)S(1)} %get-tuple-element.28), channel_id=1, source_target_pairs={{0,1},{1,2},{2,3},{3,0},{4,5},{5,6},{6,7},{7,4},{8,9},{9,10},{10,1... | collective-permute-start | bytes 4832 | tf_op jit(solution)/shard_map/ppermute | solution.py:19
  28.6 5.3 %collective-permute-start.5 = (f32[1,64,512]{2,1,0:T(8,128)S(1)}, f32[1,64,512]{2,1,0:T(8,128)S(1)}, u32[]{:S(2)}, u32[]{:S(2)}) collective-permute-start(f32[1,64,512]{2,1,0:T(8,128)S(1)} %get-tuple-element.31), channel_id=1, source_target_pairs={{4,0},{0,4},{5,1},{1,5},{6,2},{2,6},{7,3},{3,7},{12,8},{8,12},{13,... | collective-permute-start | bytes 393224 | tf_op jit(solution)/shard_map/ppermute | solution.py:21
  30.1 5.0 %collective-permute-start.4 = (f32[1,64,512]{2,1,0:T(8,128)S(1)}, f32[1,64,512]{2,1,0:T(8,128)S(1)}, u32[]{:S(2)}, u32[]{:S(2)}) collective-permute-start(f32[1,64,512]{2,1,0:T(8,128)S(1)} %get-tuple-element.30), channel_id=1, source_target_pairs={{0,4},{4,0},{1,5},{5,1},{2,6},{6,2},{3,7},{7,3},{8,12},{12,8},{9,1... | collective-permute-start | bytes 393224 | tf_op jit(solution)/shard_map/ppermute | solution.py:19
  35.1 0.6 copy-start.2
  36.5 82.4 %collective-permute-start.7 = (f32[1,256,64]{2,1,0:T(8,128)}, f32[1,256,64]{2,1,0:T(8,128)}, u32[]{:S(2)}, u32[]{:S(2)}) collective-permute-start(f32[1,256,64]{2,1,0:T(8,128)} %get-tuple-element.27), channel_id=1, source_target_pairs={{1,0},{2,1},{3,2},{0,3},{5,4},{6,5},{7,6},{4,7},{9,8},{10,9},{11,1... | collective-permute-start | bytes 196616 | tf_op jit(solution)/shard_map/ppermute | solution.py:21
  38.4 80.6 %collective-permute-start.6 = (f32[1,256,64]{2,1,0:T(8,128)}, f32[1,256,64]{2,1,0:T(8,128)}, u32[]{:S(2)}, u32[]{:S(2)}) collective-permute-start(f32[1,256,64]{2,1,0:T(8,128)} %get-tuple-element.26), channel_id=1, source_target_pairs={{0,1},{1,2},{2,3},{3,0},{4,5},{5,6},{6,7},{7,4},{8,9},{9,10},{10,1... | collective-permute-start | bytes 196616 | tf_op jit(solution)/shard_map/ppermute | solution.py:19
  106.7 12.2 %copy-start.3 = (f32[1,64,512]{2,1,0:T(8,128)S(1)}, f32[1,64,512]{2,1,0:T(8,128)}, u32[]{:S(2)}) copy-start(f32[1,64,512]{2,1,0:T(8,128)} %copy-done.2) | copy-start | bytes 393220
  106.7 13.5 %copy-start.4 = (s32[128,512]{1,0:T(8,128)S(1)}, s32[128,512]{1,0:T(8,128)}, u32[]{:S(2)}) copy-start(s32[128,512]{1,0:T(8,128)} %param.9) | copy-start | bytes 786436
  159.8 6.0 %copy-start.1 = (f32[16,8,64,8]{3,2,1,0:T(8,128)S(1)}, f32[16,8,64,8]{3,2,1,0:T(8,128)}, u32[]{:S(2)}) copy-start(f32[16,8,64,8]{3,2,1,0:T(8,128)} %mul.223) | copy-start | bytes 786436
  165.8 5.1 %copy-start = (f32[16,8,64,8]{3,2,1,0:T(8,128)S(1)}, f32[16,8,64,8]{3,2,1,0:T(8,128)}, u32[]{:S(2)}) copy-start(f32[16,8,64,8]{3,2,1,0:T(8,128)} %mul.227) | copy-start | bytes 786436
  165.8 10.1 %slice-start.6 = ((s8[8388608]{0:T(1024)(128)(4,1)}), s8[4194304]{0:T(1024)(128)(4,1)S(1)}, s32[]{:S(2)}) async-start(s8[8388608]{0:T(1024)(128)(4,1)} %bitcast.106), calls=%async_computation.7 | async-start | bytes 8388608
  170.9 5.1 %slice-start.7 = ((s8[8388608]{0:T(1024)(128)(4,1)}), s8[4194304]{0:T(1024)(128)(4,1)S(1)}, s32[]{:S(2)}) async-start(s8[8388608]{0:T(1024)(128)(4,1)} %bitcast.106), calls=%async_computation.8 | async-start | bytes 8388608
  170.9 8.9 %slice-start.4 = ((s8[8388608]{0:T(1024)(128)(4,1)}), s8[4194304]{0:T(1024)(128)(4,1)S(1)}, s32[]{:S(2)}) async-start(s8[8388608]{0:T(1024)(128)(4,1)} %bitcast.104), calls=%async_computation.5 | async-start | bytes 8388608
  176.0 3.8 %slice-start.5 = ((s8[8388608]{0:T(1024)(128)(4,1)}), s8[4194304]{0:T(1024)(128)(4,1)S(1)}, s32[]{:S(2)}) async-start(s8[8388608]{0:T(1024)(128)(4,1)} %bitcast.104), calls=%async_computation.6 | async-start | bytes 8388608
  179.8 9.8 %slice-start.2 = ((s8[8388608]{0:T(1024)(128)(4,1)}), s8[4194304]{0:T(1024)(128)(4,1)S(1)}, s32[]{:S(2)}) async-start(s8[8388608]{0:T(1024)(128)(4,1)} %bitcast.102), calls=%async_computation.3 | async-start | bytes 8388608
  183.6 6.0 %slice-start.3 = ((s8[8388608]{0:T(1024)(128)(4,1)}), s8[4194304]{0:T(1024)(128)(4,1)S(1)}, s32[]{:S(2)}) async-start(s8[8388608]{0:T(1024)(128)(4,1)} %bitcast.102), calls=%async_computation.4 | async-start | bytes 8388608
  183.6 9.9 %slice-start = ((s8[8388608]{0:T(1024)(128)(4,1)}), s8[4194304]{0:T(1024)(128)(4,1)S(1)}, s32[]{:S(2)}) async-start(s8[8388608]{0:T(1024)(128)(4,1)} %bitcast.100), calls=%async_computation.1 | async-start | bytes 8388608
  189.6 3.8 %slice-start.1 = ((s8[8388608]{0:T(1024)(128)(4,1)}), s8[4194304]{0:T(1024)(128)(4,1)S(1)}, s32[]{:S(2)}) async-start(s8[8388608]{0:T(1024)(128)(4,1)} %bitcast.100), calls=%async_computation.2 | async-start | bytes 8388608
  197.1 0.7 copy-start.5
Sparse Core Ops, SparseCore 0:
  197.9 32.0 all-reduce.1
where the time goes:
time: 239 us; the launch traced here: 238 us
  local copies, waits for them, and re-layouts  96.4 us (40%)
  other arithmetic  53.4 us (22%)
  between operations  41.5 us (17%)
  waiting for transfers between devices  35.9 us (15%)
  starting transfers between devices  11.2 us (5%)
    convert_element_type x9, local copies, waits for them, and re-layouts, on_device(): terms = weights[d].astype(jnp.float32) * masked[None]  57.9 us
    reduce_sum x9, other arithmetic, on_device(): terms.reshape(2, rows // SUB, SUB, cols // SUB, SUB).sum(axis=(2, 4))  42.9 us
    mul x9, local copies, waits for them, and re-layouts, on_device(): terms = weights[d].astype(jnp.float32) * masked[None]  32.8 us
    psum x1, waiting for transfers between devices, on_device(): return lax.psum(local_slopes, 'layer')  32.2 us
    ppermute x4, starting transfers between devices, padded(): lax.ppermute(head, axis, [((i + 1) % count, i) for i in range(count)])  10.5 us
  transfers between devices with their start and end apart: 9, of which 3 were waited for; matrix products, arithmetic and copies ran while one was open for 27% of the time, Pallas kernels for 0%

commit v1 on v0

v1 whole, which is shorter than its diff:
```python
import functools

import jax
import jax.numpy as jnp
from jax import lax
from jax.experimental import pallas as pl
from jax.experimental.pallas import tpu as pltpu
from jax.sharding import PartitionSpec as P

DIRS = 9
SUB = 8
HMAX = 2
FOOT = 64
LANES = 128
RIM = 72
MESH = pl.DeviceIdType.MESH


def kernel(
    sizes, wind, offsets, layers, weights, sub_index, out, field, shifted, wraw, wlive, sub, parts,
    local_sem, xs_sem, xr_sem, zs_sem, zr_sem, ss_sem, sr_sem,
):
    n_layer, n_tx, n_ty = sizes
    rows, cols = sub_index.shape
    tiles = cols // LANES
    groups = rows // SUB
    last = tiles + 1
    foot_rows = RIM if n_tx > 2 else rows - RIM
    layer = lax.axis_index("layer")
    tx = lax.axis_index("tx")
    ty = lax.axis_index("ty")
    up = {"tx": lax.rem(tx + n_tx - 1, n_tx)}
    down = {"tx": lax.rem(tx + 1, n_tx)}
    left = {"ty": lax.rem(ty + n_ty - 1, n_ty)}
    right = {"ty": lax.rem(ty + 1, n_ty)}
    peers = [{"layer": lax.rem(layer + k, n_layer)} for k in range(1, n_layer)]

    own = []
    for c in range(tiles):
        copy = pltpu.make_async_copy(
            layers.at[0, :, pl.ds(c * LANES, LANES)],
            field.at[c + 1, pl.ds(RIM, rows), :],
            local_sem.at[c],
        )
        copy.start()
        own.append(copy)
    sub_copy = pltpu.make_async_copy(sub_index, sub, local_sem.at[tiles])
    sub_copy.start()
    weight_copy = pltpu.make_async_copy(weights, wraw, local_sem.at[tiles + 1])
    weight_copy.start()

    barrier = pltpu.get_barrier_semaphore()
    greeted = [up, left, right] if n_tx == 2 else [up, down, left, right]
    for device in greeted + peers:
        pl.semaphore_signal(barrier, inc=1, device_id=device, device_id_type=MESH)
    pl.semaphore_wait(barrier, len(greeted) + len(peers))

    def send(src, dst, send_sem, recv_sem, device):
        copy = pltpu.make_async_remote_copy(
            src_ref=src, dst_ref=dst, send_sem=send_sem, recv_sem=recv_sem,
            device_id=device, device_id_type=MESH,
        )
        copy.start()
        return copy

    def send_rows(c):
        return [
            send(
                field.at[c, pl.ds(rows, RIM), :], field.at[c, pl.ds(0, RIM), :],
                xs_sem.at[c - 1, 0], xr_sem.at[c - 1, 0], down,
            ),
            send(
                field.at[c, pl.ds(RIM, foot_rows), :], field.at[c, pl.ds(RIM + rows, foot_rows), :],
                xs_sem.at[c - 1, 1], xr_sem.at[c - 1, 1], up,
            ),
        ]

    def send_cols(start, size, k):
        return [
            send(
                field.at[tiles, pl.ds(start, size), :], field.at[0, pl.ds(start, size), :],
                zs_sem.at[0, k], zr_sem.at[0, k], right,
            ),
            send(
                field.at[1, pl.ds(start, size), :], field.at[last, pl.ds(start, size), :],
                zs_sem.at[1, k], zr_sem.at[1, k], left,
            ),
        ]

    for copy in own:
        copy.wait()
    edge_copies = send_rows(1) + send_rows(tiles)
    col_copies = send_cols(RIM, rows, 0)
    mid_copies = []
    for c in range(2, tiles):
        mid_copies += send_rows(c)

    sub_copy.wait()
    weight_copy.wait()

    def prepare(d, carry):
        for c in range(tiles):
            for g in range(0, groups, 2):
                live = (sub[pl.ds(g * SUB, 2 * SUB), pl.ds(c * LANES, LANES)] >= 0).astype(jnp.float32)
                for s in range(2):
                    both = wraw[d, s, pl.ds(g * SUB, 2 * SUB), pl.ds(c * LANES, LANES)].astype(jnp.float32) * live
                    for h in range(2):
                        wlive[d, s, c, pl.ds(g + h, SUB, stride=groups), :] = both[h * SUB : (h + 1) * SUB]
        return carry

    lax.fori_loop(0, 4, prepare, 0)
    for copy in edge_copies:
        copy.wait_recv()
    col_copies += send_cols(0, RIM, 1) + send_cols(RIM + rows, foot_rows, 2)
    lax.fori_loop(4, DIRS, prepare, 0)

    for copy in mid_copies:
        copy.wait_recv()
    for copy in col_copies:
        copy.wait_recv()
    if n_tx == 2:
        for c in range(tiles + 2):
            field[c, pl.ds(RIM + rows + foot_rows, RIM - foot_rows), :] = field[c, pl.ds(0, RIM - foot_rows), :]

    wide = rows // SUB + 2 * FOOT // SUB
    qrow = lax.shift_right_arithmetic(wind[0, 0], 6)
    qcol = lax.shift_right_arithmetic(wind[0, 1], 6)
    frow = (wind[0, 0] - 64 * qrow).astype(jnp.float32) / 64.0
    fcol = (wind[0, 1] - 64 * qcol).astype(jnp.float32) / 64.0
    lead = HMAX + 1 - qcol
    lane = lax.broadcasted_iota(jnp.int32, (wide, LANES), 1)

    def shift_phase(p, carry):
        mixed = []
        for c in range(tiles + 2):
            here = field[c, pl.ds(RIM - FOOT + p - qrow, wide, stride=SUB), :]
            above = field[c, pl.ds(RIM - FOOT - 1 + p - qrow, wide, stride=SUB), :]
            mixed.append((1.0 - frow) * here + frow * above)
        first = [pltpu.roll(m, (LANES - lead) & (LANES - 1), 1) for m in mixed]
        second = [pltpu.roll(m, (LANES + 1 - lead) & (LANES - 1), 1) for m in mixed]
        for c in range(tiles + 2):
            after = min(c + 1, last)
            one = jnp.where(lane < LANES - lead, first[c], first[after])
            two = jnp.where(lane < LANES + 1 - lead, second[c], second[after])
            shifted[c, p, :, :] = (1.0 - fcol) * one + fcol * two
        return carry

    lax.fori_loop(0, SUB, shift_phase, 0)

    lane_g = lax.broadcasted_iota(jnp.int32, (groups, LANES), 1)
    half = cols // SUB
    pick_row = lax.broadcasted_iota(jnp.int32, (cols, LANES), 0)
    pick_col = lax.broadcasted_iota(jnp.int32, (cols, LANES), 1)
    pick = (lax.shift_right_logical(pick_row, 3) == (pick_col & (half - 1))).astype(jnp.bfloat16)

    def slopes(d, carry):
        top = offsets[0, d, 0] + FOOT
        begin = offsets[0, d, 1] + LANES - HMAX - 1
        base = lax.shift_right_arithmetic(begin, 7)
        skip = begin & (LANES - 1)
        turn = (LANES - skip) & (LANES - 1)
        sums = [[None] * tiles for _ in range(2)]
        for r in range(SUB):
            row = top + r
            phase = row & (SUB - 1)
            first = lax.shift_right_arithmetic(row, 3)
            turned = [
                pltpu.roll(shifted[base + c, phase, pl.ds(first, groups), :], turn, 1) for c in range(tiles + 1)
            ]
            for c in range(tiles):
                view = jnp.where(lane_g < LANES - skip, turned[c], turned[c + 1])
                for s in range(2):
                    term = wlive[d, s, c, pl.ds(r * groups, groups), :] * view
                    sums[s][c] = term if r == 0 else sums[s][c] + term
        rows_of = []
        for s in range(2):
            total = jnp.concatenate(sums[s], axis=1)
            high = total.astype(jnp.bfloat16)
            low = (total - high.astype(jnp.float32)).astype(jnp.bfloat16)
            rows_of += [high, low]
        added = jnp.dot(jnp.concatenate(rows_of, axis=0), pick, preferred_element_type=jnp.float32)
        one = added[0:groups] + added[groups : 2 * groups]
        two = added[2 * groups : 3 * groups] + added[3 * groups : 4 * groups]
        parts[layer, d, :, :] = jnp.where(lane_g < half, one, two)
        return carry

    sum_copies = []
    third = DIRS // 3
    for b in range(3):
        lax.fori_loop(b * third, (b + 1) * third, slopes, 0)
        for k in range(n_layer - 1):
            block = parts.at[layer, pl.ds(b * third, third)]
            sum_copies.append(send(block, block, ss_sem.at[k, b], sr_sem.at[k, b], peers[k]))
    for copy in sum_copies:
        copy.wait_recv()
    whole = parts[0]
    for k in range(1, n_layer):
        whole = whole + parts[k]
    out[0] = whole[:, :, :half]
    out[1] = whole[:, :, half:]

    for copy in edge_copies + mid_copies + col_copies + sum_copies:
        copy.wait_send()


def on_device(sizes, layers, wind, offsets, weights, sub_index):
    rows, cols = sub_index.shape
    tiles = cols // LANES
    groups = rows // SUB
    wide = groups + 2 * FOOT // SUB
    smem = pl.BlockSpec(memory_space=pltpu.SMEM)
    hbm = pl.BlockSpec(memory_space=pl.ANY)
    return pl.pallas_call(
        functools.partial(kernel, sizes),
        out_shape=jax.ShapeDtypeStruct((2, DIRS, groups, cols // SUB), jnp.float32),
        in_specs=[smem, smem, hbm, hbm, hbm],
        out_specs=pl.BlockSpec(memory_space=pltpu.VMEM),
        scratch_shapes=[
            pltpu.VMEM((tiles + 2, rows + 2 * RIM, LANES), jnp.float32),
            pltpu.VMEM((tiles + 2, SUB, wide, LANES), jnp.float32),
            pltpu.VMEM(weights.shape, weights.dtype),
            pltpu.VMEM((DIRS, 2, tiles, rows, LANES), jnp.float32),
            pltpu.VMEM(sub_index.shape, sub_index.dtype),
            pltpu.VMEM((sizes[0], DIRS, groups, LANES), jnp.float32),
            pltpu.SemaphoreType.DMA((tiles + 2,)),
            pltpu.SemaphoreType.DMA((tiles, 2)),
            pltpu.SemaphoreType.DMA((tiles, 2)),
            pltpu.SemaphoreType.DMA((2, 3)),
            pltpu.SemaphoreType.DMA((2, 3)),
            pltpu.SemaphoreType.DMA((sizes[0] - 1, 3)),
            pltpu.SemaphoreType.DMA((sizes[0] - 1, 3)),
        ],
        compiler_params=pltpu.CompilerParams(
            collective_id=0, has_side_effects=True, vmem_limit_bytes=32 * 1024 * 1024
        ),
    )(wind, offsets, layers, weights, sub_index)


def solution(mesh):
    sizes = (mesh.shape["layer"], mesh.shape["tx"], mesh.shape["ty"])
    placed = (
        P("layer", "tx", "ty"),
        P("layer", None),
        P("layer", None, None),
        P(None, None, "tx", "ty"),
        P("tx", "ty"),
    )
    return jax.shard_map(
        functools.partial(on_device, sizes),
        mesh=mesh, in_specs=placed, out_specs=P(None, None, "tx", "ty"), check_vma=False,
    )
```

time: 239 us -> 28.7 us (0.12)
  local copies, waits for them, and re-layouts: 96.4 us -> 5.65 us
  other arithmetic: 53.4 us -> 0 us
  between operations: 41.5 us -> 0.01 us
  waiting for transfers between devices: 35.9 us -> 0 us
  Pallas kernels: 0 us -> 22.8 us
  starting transfers between devices: 11.2 us -> 0 us
    convert_element_type x9 -> x0, local copies, waits for them, and re-layouts: 57.9 us -> none  [on_device(): terms = weights[d].astype(jnp.float32) * masked[None]]
    reduce_sum x9 -> x0, other arithmetic: 42.9 us -> none  [on_device(): terms.reshape(2, rows // SUB, SUB, cols // SUB, SUB).sum(axis=(2, 4))]
    mul x9 -> x0, local copies, waits for them, and re-layouts: 32.8 us -> none  [on_device(): terms = weights[d].astype(jnp.float32) * masked[None]]
    psum x1 -> x0, waiting for transfers between devices: 32.2 us -> none  [on_device(): return lax.psum(local_slopes, 'layer')]
    pallas_call x0 -> x1, Pallas kernels: none -> 22.8 us  [on_device(): pl.pallas_call(functools.partial(kernel, sizes), out_shape=jax.ShapeDtype...]
    ppermute x8 -> x0, starting transfers between devices: 11.2 us -> none  [the longest x4 10.5 us: padded(): lax.ppermute(head, axis, [((i + 1) % count, i) for i in range(count)])]
    ppermute x8 -> x0, waiting for transfers between devices: 3.64 us -> none  [the longest x4 3.63 us: padded(): lax.ppermute(tail, axis, [(i, (i + 1) % count) for i in range(count)])]
    convert_element_type x1 -> x0, other arithmetic: 3.22 us -> none  [on_device(): terms = weights[d].astype(jnp.float32) * masked[None]]
  transfers between devices with their start and end apart: 9 -> 0, of which waited for: 3 -> 0; matrix products, arithmetic and copies ran while one was open for 27% -> 0% of each run, Pallas kernels for 0% -> 0%
where the time goes in v1:
time: 28.7 us; the launch traced here: 28.5 us
  Pallas kernels  22.8 us (79%)
  local copies, waits for them, and re-layouts  5.65 us (20%)
    pallas_call x1, Pallas kernels, on_device(): pl.pallas_call(functools.partial(kernel, sizes), out_shape=jax.ShapeDtype...  22.8 us
    unnamed x10, local copies, waits for them, and re-layouts  5.65 us

profile of v1, /device:TPU:0, one launch (start us, length us, event | category | flops | bytes accessed | tf_op | source)
XLA Modules:
  0.0 28.5 jit_solution(14254537319915440988)
XLA Ops:
  0.0 0.8 %copy.6.offsets = s32[1,9,2]{2,1,0:T(8,128)S(1)} copy(s32[1,9,2]{1,2,0:T(2,128)} %param.7) | data formatting | bytes 144 | tf_op args[2]
  0.8 0.0 copy-start
  0.8 1.7 %copy-done = bf16[9,2,128,512]{3,2,1,0:T(8,128)(2,1)S(1)} copy-done((bf16[9,2,128,512]{3,2,1,0:T(8,128)(2,1)S(1)}, bf16[9,2,128,512]{3,2,1,0:T(8,128)(2,1)}, u32[]{:S(2)}) %copy-start) | copy-done | bytes 2359320
  2.4 0.0 copy-start.1
  2.4 0.9 %copy-done.1 = f32[1,128,512]{2,1,0:T(8,128)S(1)} copy-done((f32[1,128,512]{2,1,0:T(8,128)S(1)}, f32[1,128,512]{2,1,0:T(8,128)}, u32[]{:S(2)}) %copy-start.1) | copy-done | bytes 262168
  3.4 0.0 copy-start.2
  3.4 0.9 %copy-done.2 = s32[128,512]{1,0:T(8,128)S(1)} copy-done((s32[128,512]{1,0:T(8,128)S(1)}, s32[128,512]{1,0:T(8,128)}, u32[]{:S(2)}) %copy-start.2) | copy-done | bytes 262168
  4.3 0.0 copy-start.3
  4.3 0.7 %copy-done.3 = s32[1,2]{1,0:T(1,128)S(1)} copy-done((s32[1,2]{1,0:T(1,128)S(1)}, s32[1,2]{1,0:T(1,128)}, u32[]{:S(2)}) %copy-start.3) | copy-done | bytes 32
  5.0 22.8 %shard_map.55 = f32[2,9,16,64]{3,2,1,0:T(8,128)S(1)} custom-call(s32[1,2]{1,0:T(1,128)S(1)} %copy-done.3, s32[1,9,2]{2,1,0:T(8,128)S(1)} %copy.6.offsets, f32[1,128,512]{2,1,0:T(8,128)S(1)} %copy-done.1, bf16[9,2,128,512]{3,2,1,0:T(8,128)(2,1)S(1)} %copy-done, s32[128,512]{1,0:T(8,128)S(1)} %copy-done.2), custom_call_target="tpu_custom_call" | custom-call | tf_op jit(solution)/shard_map/pallas_call | solution.py:213
  27.8 0.7 %copy.8 = f32[2,9,16,64]{3,2,1,0:T(8,128)} copy(f32[2,9,16,64]{3,2,1,0:T(8,128)S(1)} %shard_map.55) | data formatting | bytes 147456
Async XLA Ops:
  0.8 1.7 %copy-start = (bf16[9,2,128,512]{3,2,1,0:T(8,128)(2,1)S(1)}, bf16[9,2,128,512]{3,2,1,0:T(8,128)(2,1)}, u32[]{:S(2)}) copy-start(bf16[9,2,128,512]{3,2,1,0:T(8,128)(2,1)} %weights.1) | copy-start | bytes 7077892
  2.4 0.9 %copy-start.1 = (f32[1,128,512]{2,1,0:T(8,128)S(1)}, f32[1,128,512]{2,1,0:T(8,128)}, u32[]{:S(2)}) copy-start(f32[1,128,512]{2,1,0:T(8,128)} %layers.1) | copy-start | bytes 786436
  3.4 0.9 %copy-start.2 = (s32[128,512]{1,0:T(8,128)S(1)}, s32[128,512]{1,0:T(8,128)}, u32[]{:S(2)}) copy-start(s32[128,512]{1,0:T(8,128)} %sub_index.1) | copy-start | bytes 786436
  4.3 0.7 %copy-start.3 = (s32[1,2]{1,0:T(1,128)S(1)}, s32[1,2]{1,0:T(1,128)}, u32[]{:S(2)}) copy-start(s32[1,2]{1,0:T(1,128)} %wind.1) | copy-start | bytes 28

commit v2 on v1

--- a/solution.py
+++ b/solution.py
@@ -154,8 +154,8 @@
     pick = (lax.shift_right_logical(pick_row, 3) == (pick_col & (half - 1))).astype(jnp.bfloat16)
 
     def slopes(d, carry):
-        top = offsets[0, d, 0] + FOOT
-        begin = offsets[0, d, 1] + LANES - HMAX - 1
+        top = offsets[0, 0, d] + FOOT
+        begin = offsets[0, 1, d] + LANES - HMAX - 1
         base = lax.shift_right_arithmetic(begin, 7)
         skip = begin & (LANES - 1)
         turn = (LANES - skip) & (LANES - 1)
@@ -209,7 +209,7 @@
     groups = rows // SUB
     wide = groups + 2 * FOOT // SUB
     smem = pl.BlockSpec(memory_space=pltpu.SMEM)
-    hbm = pl.BlockSpec(memory_space=pl.ANY)
+    hbm = pl.BlockSpec(memory_space=pltpu.HBM)
     return pl.pallas_call(
         functools.partial(kernel, sizes),
         out_shape=jax.ShapeDtypeStruct((2, DIRS, groups, cols // SUB), jnp.float32),
@@ -231,9 +231,9 @@
             pltpu.SemaphoreType.DMA((sizes[0] - 1, 3)),
         ],
         compiler_params=pltpu.CompilerParams(
-            collective_id=0, has_side_effects=True, vmem_limit_bytes=32 * 1024 * 1024
+            collective_id=0, has_side_effects=True, vmem_limit_bytes=60 * 1024 * 1024
         ),
-    )(wind, offsets, layers, weights, sub_index)
+    )(wind, jnp.swapaxes(offsets, 1, 2), layers, weights, sub_index)
 
 
 def solution(mesh):

time: 28.7 us -> 25.4 us (0.89)
  local copies, waits for them, and re-layouts: 5.65 us -> 1.58 us
  Pallas kernels: 22.8 us -> 23.6 us
    unnamed x10 -> x1, local copies, waits for them, and re-layouts: 5.65 us -> 1.58 us
    pallas_call x1, Pallas kernels: 22.8 us -> 23.6 us  [on_device(): pl.pallas_call(functools.partial(kernel, sizes), out_shape=jax.ShapeDtype...]
where the time goes in v2:
time: 25.4 us; the launch traced here: 25.2 us
  Pallas kernels  23.6 us (93%)
  local copies, waits for them, and re-layouts  1.58 us (6%)
    pallas_call x1, Pallas kernels, on_device(): pl.pallas_call(functools.partial(kernel, sizes), out_shape=jax.ShapeDtype...  23.6 us
    unnamed x1, local copies, waits for them, and re-layouts  1.58 us

profile of v2, /device:TPU:0, one launch (start us, length us, event | category | flops | bytes accessed | tf_op | source)
XLA Modules:
  0.0 25.2 jit_solution(5811401767365595978)
XLA Ops:
  0.0 23.6 %shard_map.55 = f32[2,9,16,64]{3,2,1,0:T(8,128)} custom-call(s32[1,2]{1,0:T(1,128)} %wind.1, s32[1,2,9]{2,1,0:T(2,128)} %bitcast.1, f32[1,128,512]{2,1,0:T(8,128)} %layers.1, bf16[9,2,128,512]{3,2,1,0:T(8,128)(2,1)} %weights.1, s32[128,512]{1,0:T(8,128)} %sub_index.1), custom_call_target="tpu_custom_call" | custom-call | tf_op jit(solution)/shard_map/pallas_call | solution.py:213
  23.7 1.6 %copy.7 = f32[2,9,16,64]{3,2,1,0:T(8,128)} copy(f32[2,9,16,64]{3,2,1,0:T(8,128)} %shard_map.55) | data formatting | bytes 147456

commit v3 on v2

--- a/solution.py
+++ b/solution.py
@@ -17,7 +17,7 @@
 
 
 def kernel(
-    sizes, wind, offsets, layers, weights, sub_index, out, field, shifted, wraw, wlive, sub, parts,
+    sizes, wind, offsets, layers, weights, sub_index, out, field, side, shifted, wraw, wlive, sub, parts,
     local_sem, xs_sem, xr_sem, zs_sem, zr_sem, ss_sem, sr_sem,
 ):
     n_layer, n_tx, n_ty = sizes
@@ -35,19 +35,15 @@
     right = {"ty": lax.rem(ty + 1, n_ty)}
     peers = [{"layer": lax.rem(layer + k, n_layer)} for k in range(1, n_layer)]
 
-    own = []
-    for c in range(tiles):
-        copy = pltpu.make_async_copy(
+    order = [0, tiles - 1] + list(range(1, tiles - 1))
+    own = {}
+    for c in order:
+        own[c] = pltpu.make_async_copy(
             layers.at[0, :, pl.ds(c * LANES, LANES)],
-            field.at[c + 1, pl.ds(RIM, rows), :],
+            field.at[c, pl.ds(RIM, rows), :],
             local_sem.at[c],
         )
-        copy.start()
-        own.append(copy)
-    sub_copy = pltpu.make_async_copy(sub_index, sub, local_sem.at[tiles])
-    sub_copy.start()
-    weight_copy = pltpu.make_async_copy(weights, wraw, local_sem.at[tiles + 1])
-    weight_copy.start()
+        own[c].start()
 
     barrier = pltpu.get_barrier_semaphore()
     greeted = [up, left, right] if n_tx == 2 else [up, down, left, right]
@@ -67,34 +63,39 @@
         return [
             send(
                 field.at[c, pl.ds(rows, RIM), :], field.at[c, pl.ds(0, RIM), :],
-                xs_sem.at[c - 1, 0], xr_sem.at[c - 1, 0], down,
+                xs_sem.at[c, 0], xr_sem.at[c, 0], down,
             ),
             send(
                 field.at[c, pl.ds(RIM, foot_rows), :], field.at[c, pl.ds(RIM + rows, foot_rows), :],
-                xs_sem.at[c - 1, 1], xr_sem.at[c - 1, 1], up,
+                xs_sem.at[c, 1], xr_sem.at[c, 1], up,
             ),
         ]
 
     def send_cols(start, size, k):
         return [
             send(
-                field.at[tiles, pl.ds(start, size), :], field.at[0, pl.ds(start, size), :],
+                field.at[tiles - 1, pl.ds(start, size), :], side.at[0, pl.ds(start, size), :],
                 zs_sem.at[0, k], zr_sem.at[0, k], right,
             ),
             send(
-                field.at[1, pl.ds(start, size), :], field.at[last, pl.ds(start, size), :],
+                field.at[0, pl.ds(start, size), :], side.at[1, pl.ds(start, size), :],
                 zs_sem.at[1, k], zr_sem.at[1, k], left,
             ),
         ]
 
-    for copy in own:
-        copy.wait()
-    edge_copies = send_rows(1) + send_rows(tiles)
+    edge_copies, mid_copies = [], []
+    for c in order[:2]:
+        own[c].wait()
+        edge_copies += send_rows(c)
     col_copies = send_cols(RIM, rows, 0)
-    mid_copies = []
-    for c in range(2, tiles):
+    for c in order[2:]:
+        own[c].wait()
         mid_copies += send_rows(c)
 
+    sub_copy = pltpu.make_async_copy(sub_index, sub, local_sem.at[tiles])
+    sub_copy.start()
+    weight_copy = pltpu.make_async_copy(weights, wraw, local_sem.at[tiles + 1])
+    weight_copy.start()
     sub_copy.wait()
     weight_copy.wait()
 
@@ -114,13 +115,10 @@
     col_copies += send_cols(0, RIM, 1) + send_cols(RIM + rows, foot_rows, 2)
     lax.fori_loop(4, DIRS, prepare, 0)
 
-    for copy in mid_copies:
-        copy.wait_recv()
-    for copy in col_copies:
-        copy.wait_recv()
-    if n_tx == 2:
-        for c in range(tiles + 2):
-            field[c, pl.ds(RIM + rows + foot_rows, RIM - foot_rows), :] = field[c, pl.ds(0, RIM - foot_rows), :]
+    def fill_foot(ref, count):
+        if n_tx == 2:
+            for c in range(count):
+                ref[c, pl.ds(RIM + rows + foot_rows, RIM - foot_rows), :] = ref[c, pl.ds(0, RIM - foot_rows), :]
 
     wide = rows // SUB + 2 * FOOT // SUB
     qrow = lax.shift_right_arithmetic(wind[0, 0], 6)
@@ -130,22 +128,26 @@
     lead = HMAX + 1 - qcol
     lane = lax.broadcasted_iota(jnp.int32, (wide, LANES), 1)
 
-    def shift_phase(p, carry):
-        mixed = []
-        for c in range(tiles + 2):
-            here = field[c, pl.ds(RIM - FOOT + p - qrow, wide, stride=SUB), :]
-            above = field[c, pl.ds(RIM - FOOT - 1 + p - qrow, wide, stride=SUB), :]
-            mixed.append((1.0 - frow) * here + frow * above)
-        first = [pltpu.roll(m, (LANES - lead) & (LANES - 1), 1) for m in mixed]
-        second = [pltpu.roll(m, (LANES + 1 - lead) & (LANES - 1), 1) for m in mixed]
-        for c in range(tiles + 2):
-            after = min(c + 1, last)
-            one = jnp.where(lane < LANES - lead, first[c], first[after])
-            two = jnp.where(lane < LANES + 1 - lead, second[c], second[after])
-            shifted[c, p, :, :] = (1.0 - fcol) * one + fcol * two
-        return carry
-
-    lax.fori_loop(0, SUB, shift_phase, 0)
+    def mixed_rows(c, p):
+        ref, at = (side, 0) if c == 0 else (side, 1) if c == last else (field, c - 1)
+        here = ref[at, pl.ds(RIM - FOOT + p - qrow, wide, stride=SUB), :]
+        above = ref[at, pl.ds(RIM - FOOT - 1 + p - qrow, wide, stride=SUB), :]
+        return (1.0 - frow) * here + frow * above
+
+    def shift_tiles(pairs):
+        def phase(p, carry):
+            first, second = {}, {}
+            for c in sorted({c for pair in pairs for c in pair}):
+                m = mixed_rows(c, p)
+                first[c] = pltpu.roll(m, (LANES - lead) & (LANES - 1), 1)
+                second[c] = pltpu.roll(m, (LANES + 1 - lead) & (LANES - 1), 1)
+            for c, after in pairs:
+                one = jnp.where(lane < LANES - lead, first[c], first[after])
+                two = jnp.where(lane < LANES + 1 - lead, second[c], second[after])
+                shifted[c, p, :, :] = (1.0 - fcol) * one + fcol * two
+            return carry
+
+        lax.fori_loop(0, SUB, phase, 0)
 
     lane_g = lax.broadcasted_iota(jnp.int32, (groups, LANES), 1)
     half = cols // SUB
@@ -153,41 +155,53 @@
     pick_col = lax.broadcasted_iota(jnp.int32, (cols, LANES), 1)
     pick = (lax.shift_right_logical(pick_row, 3) == (pick_col & (half - 1))).astype(jnp.bfloat16)
 
-    def slopes(d, carry):
+    def slopes(chosen, fresh, d, carry):
+        picked = jnp.concatenate([pick[c * LANES : (c + 1) * LANES] for c in chosen], axis=0)
         top = offsets[0, 0, d] + FOOT
         begin = offsets[0, 1, d] + LANES - HMAX - 1
         base = lax.shift_right_arithmetic(begin, 7)
         skip = begin & (LANES - 1)
         turn = (LANES - skip) & (LANES - 1)
-        sums = [[None] * tiles for _ in range(2)]
+        needed = sorted(set(chosen) | {c + 1 for c in chosen})
+        sums = [{}, {}]
         for r in range(SUB):
             row = top + r
             phase = row & (SUB - 1)
             first = lax.shift_right_arithmetic(row, 3)
-            turned = [
-                pltpu.roll(shifted[base + c, phase, pl.ds(first, groups), :], turn, 1) for c in range(tiles + 1)
-            ]
-            for c in range(tiles):
+            turned = {c: pltpu.roll(shifted[base + c, phase, pl.ds(first, groups), :], turn, 1) for c in needed}
+            for c in chosen:
                 view = jnp.where(lane_g < LANES - skip, turned[c], turned[c + 1])
                 for s in range(2):
                     term = wlive[d, s, c, pl.ds(r * groups, groups), :] * view
                     sums[s][c] = term if r == 0 else sums[s][c] + term
         rows_of = []
         for s in range(2):
-            total = jnp.concatenate(sums[s], axis=1)
+            total = jnp.concatenate([sums[s][c] for c in chosen], axis=1)
             high = total.astype(jnp.bfloat16)
             low = (total - high.astype(jnp.float32)).astype(jnp.bfloat16)
             rows_of += [high, low]
-        added = jnp.dot(jnp.concatenate(rows_of, axis=0), pick, preferred_element_type=jnp.float32)
+        added = jnp.dot(jnp.concatenate(rows_of, axis=0), picked, preferred_element_type=jnp.float32)
         one = added[0:groups] + added[groups : 2 * groups]
         two = added[2 * groups : 3 * groups] + added[3 * groups : 4 * groups]
-        parts[layer, d, :, :] = jnp.where(lane_g < half, one, two)
+        slope = jnp.where(lane_g < half, one, two)
+        parts[layer, d, :, :] = slope if fresh else parts[layer, d, :, :] + slope
         return carry
+
+    for copy in mid_copies:
+        copy.wait_recv()
+    fill_foot(field, tiles)
+    shift_tiles([(c, min(c + 1, tiles)) for c in range(1, tiles + 1)])
+    lax.fori_loop(0, DIRS, functools.partial(slopes, list(range(1, tiles - 1)), True), 0)
+
+    for copy in col_copies:
+        copy.wait_recv()
+    fill_foot(side, 2)
+    shift_tiles([(0, 1), (tiles, last), (last, last)])
 
     sum_copies = []
     third = DIRS // 3
     for b in range(3):
-        lax.fori_loop(b * third, (b + 1) * third, slopes, 0)
+        lax.fori_loop(b * third, (b + 1) * third, functools.partial(slopes, [0, tiles - 1], False), 0)
         for k in range(n_layer - 1):
             block = parts.at[layer, pl.ds(b * third, third)]
             sum_copies.append(send(block, block, ss_sem.at[k, b], sr_sem.at[k, b], peers[k]))
@@ -216,7 +230,8 @@
         in_specs=[smem, smem, hbm, hbm, hbm],
         out_specs=pl.BlockSpec(memory_space=pltpu.VMEM),
         scratch_shapes=[
-            pltpu.VMEM((tiles + 2, rows + 2 * RIM, LANES), jnp.float32),
+            pltpu.VMEM((tiles, rows + 2 * RIM, LANES), jnp.float32),
+            pltpu.VMEM((2, rows + 2 * RIM, LANES), jnp.float32),
             pltpu.VMEM((tiles + 2, SUB, wide, LANES), jnp.float32),
             pltpu.VMEM(weights.shape, weights.dtype),
             pltpu.VMEM((DIRS, 2, tiles, rows, LANES), jnp.float32),

time: 25.4 us -> 26 us (1.024)
  Pallas kernels: 23.6 us -> 24.2 us
    pallas_call x1, Pallas kernels: 23.6 us -> 24.2 us  [on_device(): pl.pallas_call(functools.partial(kernel, sizes), out_shape=jax.ShapeDtype...]
where the time goes in v3:
time: 26 us; the launch traced here: 25.8 us
  Pallas kernels  24.2 us (93%)
  local copies, waits for them, and re-layouts  1.58 us (6%)
    pallas_call x1, Pallas kernels, on_device(): pl.pallas_call(functools.partial(kernel, sizes), out_shape=jax.ShapeDtype...  24.2 us
    unnamed x1, local copies, waits for them, and re-layouts  1.58 us

profile of v3, /device:TPU:0, one launch (start us, length us, event | category | flops | bytes accessed | tf_op | source)
XLA Modules:
  0.0 25.8 jit_solution(3587391740180267739)
XLA Ops:
  0.0 24.2 %shard_map.55 = f32[2,9,16,64]{3,2,1,0:T(8,128)} custom-call(s32[1,2]{1,0:T(1,128)} %wind.1, s32[1,2,9]{2,1,0:T(2,128)} %bitcast.1, f32[1,128,512]{2,1,0:T(8,128)} %layers.1, bf16[9,2,128,512]{3,2,1,0:T(8,128)(2,1)} %weights.1, s32[128,512]{1,0:T(8,128)} %sub_index.1), custom_call_target="tpu_custom_call" | custom-call | tf_op jit(solution)/shard_map/pallas_call | solution.py:227
  24.3 1.6 %copy.7 = f32[2,9,16,64]{3,2,1,0:T(8,128)} copy(f32[2,9,16,64]{3,2,1,0:T(8,128)} %shard_map.55) | data formatting | bytes 147456

commit v4 on v3

--- a/solution.py
+++ b/solution.py
@@ -45,6 +45,11 @@
         )
         own[c].start()
 
+    sub_copy = pltpu.make_async_copy(sub_index, sub, local_sem.at[tiles])
+    sub_copy.start()
+    weight_copy = pltpu.make_async_copy(weights, wraw, local_sem.at[tiles + 1])
+    weight_copy.start()
+
     barrier = pltpu.get_barrier_semaphore()
     greeted = [up, left, right] if n_tx == 2 else [up, down, left, right]
     for device in greeted + peers:
@@ -92,10 +97,6 @@
         own[c].wait()
         mid_copies += send_rows(c)
 
-    sub_copy = pltpu.make_async_copy(sub_index, sub, local_sem.at[tiles])
-    sub_copy.start()
-    weight_copy = pltpu.make_async_copy(weights, wraw, local_sem.at[tiles + 1])
-    weight_copy.start()
     sub_copy.wait()
     weight_copy.wait()
 

time: 26 us -> 26 us (level)
  no operation moved by 1% of the time
where the time goes in v4:
time: 26 us; the launch traced here: 25.8 us
  Pallas kernels  24.3 us (93%)
  local copies, waits for them, and re-layouts  1.58 us (6%)
    pallas_call x1, Pallas kernels, on_device(): pl.pallas_call(functools.partial(kernel, sizes), out_shape=jax.ShapeDtype...  24.3 us
    unnamed x1, local copies, waits for them, and re-layouts  1.58 us

profile of v4, /device:TPU:0, one launch (start us, length us, event | category | flops | bytes accessed | tf_op | source)
XLA Modules:
  0.0 25.8 jit_solution(6492540192913106832)
XLA Ops:
  0.0 24.3 %shard_map.55 = f32[2,9,16,64]{3,2,1,0:T(8,128)} custom-call(s32[1,2]{1,0:T(1,128)} %wind.1, s32[1,2,9]{2,1,0:T(2,128)} %bitcast.1, f32[1,128,512]{2,1,0:T(8,128)} %layers.1, bf16[9,2,128,512]{3,2,1,0:T(8,128)(2,1)} %weights.1, s32[128,512]{1,0:T(8,128)} %sub_index.1), custom_call_target="tpu_custom_call" | custom-call | tf_op jit(solution)/shard_map/pallas_call | solution.py:228
  24.3 1.6 %copy.7 = f32[2,9,16,64]{3,2,1,0:T(8,128)} copy(f32[2,9,16,64]{3,2,1,0:T(8,128)} %shard_map.55) | data formatting | bytes 147456

commit v5 on v2

--- a/solution.py
+++ b/solution.py
@@ -35,15 +35,16 @@
     right = {"ty": lax.rem(ty + 1, n_ty)}
     peers = [{"layer": lax.rem(layer + k, n_layer)} for k in range(1, n_layer)]
 
-    own = []
-    for c in range(tiles):
+    order = [0, tiles - 1] + list(range(1, tiles - 1))
+    own = {}
+    for c in order:
         copy = pltpu.make_async_copy(
             layers.at[0, :, pl.ds(c * LANES, LANES)],
             field.at[c + 1, pl.ds(RIM, rows), :],
             local_sem.at[c],
         )
         copy.start()
-        own.append(copy)
+        own[c] = copy
     sub_copy = pltpu.make_async_copy(sub_index, sub, local_sem.at[tiles])
     sub_copy.start()
     weight_copy = pltpu.make_async_copy(weights, wraw, local_sem.at[tiles + 1])
@@ -87,13 +88,14 @@
             ),
         ]
 
-    for copy in own:
-        copy.wait()
-    edge_copies = send_rows(1) + send_rows(tiles)
+    edge_copies, mid_copies = [], []
+    for c in order[:2]:
+        own[c].wait()
+        edge_copies += send_rows(c + 1)
     col_copies = send_cols(RIM, rows, 0)
-    mid_copies = []
-    for c in range(2, tiles):
-        mid_copies += send_rows(c)
+    for c in order[2:]:
+        own[c].wait()
+        mid_copies += send_rows(c + 1)
 
     sub_copy.wait()
     weight_copy.wait()
@@ -185,11 +187,11 @@
         return carry
 
     sum_copies = []
-    third = DIRS // 3
+    cuts = [0, 4, 7, DIRS]
     for b in range(3):
-        lax.fori_loop(b * third, (b + 1) * third, slopes, 0)
+        lax.fori_loop(cuts[b], cuts[b + 1], slopes, 0)
         for k in range(n_layer - 1):
-            block = parts.at[layer, pl.ds(b * third, third)]
+            block = parts.at[layer, pl.ds(cuts[b], cuts[b + 1] - cuts[b])]
             sum_copies.append(send(block, block, ss_sem.at[k, b], sr_sem.at[k, b], peers[k]))
     for copy in sum_copies:
         copy.wait_recv()

time: 25.4 us -> 25.2 us (level)
  no operation moved by 1% of the time
where the time goes in v5:
time: 25.2 us; the launch traced here: 25.1 us
  Pallas kernels  23.5 us (93%)
  local copies, waits for them, and re-layouts  1.58 us (6%)
    pallas_call x1, Pallas kernels, on_device(): pl.pallas_call(functools.partial(kernel, sizes), out_shape=jax.ShapeDtype...  23.5 us
    unnamed x1, local copies, waits for them, and re-layouts  1.58 us

profile of v5, /device:TPU:0, one launch (start us, length us, event | category | flops | bytes accessed | tf_op | source)
XLA Modules:
  0.0 25.1 jit_solution(1144345501949570825)
XLA Ops:
  0.0 23.5 %shard_map.55 = f32[2,9,16,64]{3,2,1,0:T(8,128)} custom-call(s32[1,2]{1,0:T(1,128)} %wind.1, s32[1,2,9]{2,1,0:T(2,128)} %bitcast.1, f32[1,128,512]{2,1,0:T(8,128)} %layers.1, bf16[9,2,128,512]{3,2,1,0:T(8,128)(2,1)} %weights.1, s32[128,512]{1,0:T(8,128)} %sub_index.1), custom_call_target="tpu_custom_call" | custom-call | tf_op jit(solution)/shard_map/pallas_call | solution.py:215
  23.5 1.6 %copy.7 = f32[2,9,16,64]{3,2,1,0:T(8,128)} copy(f32[2,9,16,64]{3,2,1,0:T(8,128)} %shard_map.55) | data formatting | bytes 147456

commit v6 on v5

--- a/solution.py
+++ b/solution.py
@@ -12,6 +12,7 @@
 HMAX = 2
 FOOT = 64
 LANES = 128
+CUTS = (0, 1, 3, 5, 7, DIRS)
 RIM = 72
 MESH = pl.DeviceIdType.MESH
 
@@ -187,8 +188,8 @@
         return carry
 
     sum_copies = []
-    cuts = [0, 4, 7, DIRS]
-    for b in range(3):
+    cuts = CUTS
+    for b in range(len(cuts) - 1):
         lax.fori_loop(cuts[b], cuts[b + 1], slopes, 0)
         for k in range(n_layer - 1):
             block = parts.at[layer, pl.ds(cuts[b], cuts[b + 1] - cuts[b])]
@@ -229,8 +230,8 @@
             pltpu.SemaphoreType.DMA((tiles, 2)),
             pltpu.SemaphoreType.DMA((2, 3)),
             pltpu.SemaphoreType.DMA((2, 3)),
-            pltpu.SemaphoreType.DMA((sizes[0] - 1, 3)),
-            pltpu.SemaphoreType.DMA((sizes[0] - 1, 3)),
+            pltpu.SemaphoreType.DMA((sizes[0] - 1, len(CUTS) - 1)),
+            pltpu.SemaphoreType.DMA((sizes[0] - 1, len(CUTS) - 1)),
         ],
         compiler_params=pltpu.CompilerParams(
             collective_id=0, has_side_effects=True, vmem_limit_bytes=60 * 1024 * 1024

time: 25.2 us -> 25.3 us (level)
  no operation moved by 1% of the time
where the time goes in v6:
time: 25.3 us; the launch traced here: 25.1 us
  Pallas kernels  23.6 us (93%)
  local copies, waits for them, and re-layouts  1.58 us (6%)
    pallas_call x1, Pallas kernels, on_device(): pl.pallas_call(functools.partial(kernel, sizes), out_shape=jax.ShapeDtype...  23.6 us
    unnamed x1, local copies, waits for them, and re-layouts  1.58 us

profile of v6, /device:TPU:0, one launch (start us, length us, event | category | flops | bytes accessed | tf_op | source)
XLA Modules:
  0.0 25.1 jit_solution(8230527956124039727)
XLA Ops:
  0.0 23.6 %shard_map.55 = f32[2,9,16,64]{3,2,1,0:T(8,128)} custom-call(s32[1,2]{1,0:T(1,128)} %wind.1, s32[1,2,9]{2,1,0:T(2,128)} %bitcast.1, f32[1,128,512]{2,1,0:T(8,128)} %layers.1, bf16[9,2,128,512]{3,2,1,0:T(8,128)(2,1)} %weights.1, s32[128,512]{1,0:T(8,128)} %sub_index.1), custom_call_target="tpu_custom_call" | custom-call | tf_op jit(solution)/shard_map/pallas_call | solution.py:216
  23.6 1.6 %copy.7 = f32[2,9,16,64]{3,2,1,0:T(8,128)} copy(f32[2,9,16,64]{3,2,1,0:T(8,128)} %shard_map.55) | data formatting | bytes 147456

commit v7 on v6

--- a/solution.py
+++ b/solution.py
@@ -93,10 +93,10 @@
     for c in order[:2]:
         own[c].wait()
         edge_copies += send_rows(c + 1)
-    col_copies = send_cols(RIM, rows, 0)
     for c in order[2:]:
         own[c].wait()
         mid_copies += send_rows(c + 1)
+    col_copies = send_cols(RIM, rows, 0)
 
     sub_copy.wait()
     weight_copy.wait()

time: 25.3 us -> 25.3 us (level)
  no operation moved by 1% of the time
where the time goes in v7:
time: 25.3 us; the launch traced here: 25.2 us
  Pallas kernels  23.6 us (93%)
  local copies, waits for them, and re-layouts  1.58 us (6%)
    pallas_call x1, Pallas kernels, on_device(): pl.pallas_call(functools.partial(kernel, sizes), out_shape=jax.ShapeDtype...  23.6 us
    unnamed x1, local copies, waits for them, and re-layouts  1.58 us

profile of v7, /device:TPU:0, one launch (start us, length us, event | category | flops | bytes accessed | tf_op | source)
XLA Modules:
  0.0 25.2 jit_solution(4581215831867281713)
XLA Ops:
  0.0 23.6 %shard_map.55 = f32[2,9,16,64]{3,2,1,0:T(8,128)} custom-call(s32[1,2]{1,0:T(1,128)} %wind.1, s32[1,2,9]{2,1,0:T(2,128)} %bitcast.1, f32[1,128,512]{2,1,0:T(8,128)} %layers.1, bf16[9,2,128,512]{3,2,1,0:T(8,128)(2,1)} %weights.1, s32[128,512]{1,0:T(8,128)} %sub_index.1), custom_call_target="tpu_custom_call" | custom-call | tf_op jit(solution)/shard_map/pallas_call | solution.py:216
  23.6 1.6 %copy.7 = f32[2,9,16,64]{3,2,1,0:T(8,128)} copy(f32[2,9,16,64]{3,2,1,0:T(8,128)} %shard_map.55) | data formatting | bytes 147456
